TPU v7x, 32 devices: a whole 2x2x4 slice. The times are simulated.
32 devices in a mesh: groups: 2 (over y), tensor: 4 (over z), store: 4 (over x, core).
Axes of the slice: x: 2, y: 2, z: 4, core: 2. Of those that a mesh axis runs over, the one named last changes fastest.
Arguments:
- gate: bfloat16 [768, 28672], P(('groups', 'store'), 'tensor'), parts along dimension 0, may hold values from -6 to 6
- up: bfloat16 [768, 28672], P(('groups', 'store'), 'tensor'), parts along dimension 0, may hold values from -6 to 6
- down_weight: bfloat16 [28672, 8192], P('tensor', 'store'), may hold values from -0.03125 to 0.03125
- shrink_weights: bfloat16 [32, 28672, 64], P('store', 'tensor'), may hold values from -0.03125 to 0.03125
- expand_weights: bfloat16 [32, 64, 8192], P(None, 'tensor', 'store'), may hold values from -0.75 to 0.75
- row_adapter_index: int32 [768, 1], P('groups'), parts along dimension 0, may hold values from 0 to 31; in each aligned block of 96 rows (0 to 95, 96 to 191, ...) at most 4 rows name the same one
- residual: bfloat16 [768, 8192], P(('groups', 'tensor'), 'store'), parts along dimension 0, may hold values from -6 to 6
Outputs:
- mixed: bfloat16 [768, 8192], P(('groups', 'tensor'), 'store'), parts along dimension 0
There are 2 independent parts, one for each index of `groups`. A program takes and returns all parts, laid end to end along the dimension named above; an argument that names none is the same for every part. Nothing has to cross between parts.
Inputs may be any that keep to these rules, and one draw needn't show every extreme that they name: `row_adapter_index`: in each aligned block of 96 rows no adapter is named by more than 4 rows.
All inputs are finite; a program needn't handle non-finite values.
Results may differ from a plain program's by a relative error of at most 0.0043.
Values may be sent and summed in bfloat16 or wider, within the bound.
A program may use at most 192 MiB of HBM per device.

v0:
```python
import jax
import jax.numpy as jnp
from jax import lax
from jax.sharding import PartitionSpec as P

MOST = 4


def shards(gate, up, down_weight, shrink_weights, expand_weights, row_adapter_index, residual):
    hidden = (jax.nn.silu(gate.astype(jnp.float32)) * up.astype(jnp.float32)).astype(jnp.bfloat16)
    rows_here = gate.shape[0]
    ffd = gate.shape[1]
    rank_position = shrink_weights.shape[2]
    adapter_table = expand_weights.shape[0]
    device_rank = expand_weights.shape[1]
    slots = adapter_table * MOST
    all_ids = row_adapter_index[:, 0]
    my_ids = lax.dynamic_slice_in_dim(all_ids, lax.axis_index("store") * rows_here, rows_here)
    onehot = (my_ids[:, None] == jnp.arange(adapter_table, dtype=jnp.int32)[None, :]).astype(
        jnp.int32
    )
    before = jnp.cumsum(onehot, axis=0) - onehot
    position = jnp.sum(before * onehot, axis=1)
    dest = my_ids * MOST + position
    place = (dest[:, None] == jnp.arange(slots, dtype=jnp.int32)[None, :]).astype(jnp.bfloat16)
    packed = jnp.einsum("rs,rf->sf", place, hidden, preferred_element_type=jnp.float32).astype(
        jnp.bfloat16
    )
    partial_piece = lax.all_gather(shrink_weights, "store", axis=0, tiled=True)
    count = partial_piece.shape[0]
    block = packed.reshape(count, MOST, ffd)
    part = jnp.einsum("amf,afr->amr", block, partial_piece, preferred_element_type=jnp.float32)
    shrink_slots = part.reshape(count * MOST, rank_position)
    partial_value = jnp.take(shrink_slots, dest, axis=0)
    summed = lax.psum(partial_value, "tensor")
    mine = lax.dynamic_slice_in_dim(summed, lax.axis_index("tensor") * device_rank, device_rank, 1)
    shrink_low = mine.astype(jnp.bfloat16)
    hidden_all, shrink_all = (
        lax.all_gather(hidden, "store", axis=0, tiled=True),
        lax.all_gather(shrink_low, "store", axis=0, tiled=True),
    )
    flattened_expand = expand_weights.reshape(adapter_table * device_rank, expand_weights.shape[2])
    rows_out = residual.shape[0]
    select = (all_ids[:, None] == jnp.arange(adapter_table, dtype=jnp.int32)[None, :]).astype(
        jnp.bfloat16
    )
    expand_in = (select[:, :, None] * shrink_all[:, None, :]).reshape(
        rows_out * lax.axis_size("tensor"), adapter_table * device_rank
    )
    base = jnp.dot(hidden_all, down_weight, preferred_element_type=jnp.float32)
    total = lax.psum_scatter(
        base + jnp.dot(expand_in, flattened_expand, preferred_element_type=jnp.float32),
        "tensor",
        scatter_dimension=0,
        tiled=True,
    )
    return (residual.astype(jnp.float32) + total).astype(jnp.bfloat16)


def solution(mesh):
    in_specs = (
        P(("groups", "store"), "tensor"),
        P(("groups", "store"), "tensor"),
        P("tensor", "store"),
        P("store", "tensor", None),
        P(None, "tensor", "store"),
        P("groups", None),
        P(("groups", "tensor"), "store"),
    )
    out_specs = P(("groups", "tensor"), "store")
    return jax.shard_map(shards, mesh=mesh, in_specs=in_specs, out_specs=out_specs, check_vma=False)
```

profile of v0, /device:TPU:2, one launch (start us, length us, event | category | flops | bytes accessed | tf_op | source)
XLA Modules:
  0.0 344.0 jit_solution(9245656367239299261)
XLA Ops:
  6.5 0.0 copy-start
  6.5 0.0 all-gather.4.cloned.1.call-start
  6.5 3.8 %fusion.4 = bf16[96,7168]{1,0:T(8,128)(2,1)} fusion(bf16[96,7168]{1,0:T(8,128)(2,1)} %param.8, bf16[96,7168]{1,0:T(8,128)(2,1)} %param.7), kind=kLoop, calls=%fused_computation.9 | loop fusion | flops 5505024 | bytes 4128768 | tf_op jit(solution)/shard_map/convert_element_type | solution.py:10
  10.3 0.0 all-gather.4.cloned.1.call-update
  10.4 0.0 copy-start.3
  10.4 0.0 copy-start.1
  10.4 0.0 all-gather.6.cloned.1.call-start
  10.4 0.7 all-gather.6.cloned.1.call-update
  11.1 0.0 reduce-scatter.2.cloned.1.call-start
  11.2 0.0 copy-done.3
  11.2 0.1 fusion.13
  11.3 0.7 fusion.9
  12.0 0.9 reduce_window_sum.11
  12.9 0.2 select_reduce_fusion
  13.1 0.1 and_bitcast_fusion
  13.2 0.0 copy-done.1
  13.2 2.0 convolution_convert_fusion
  15.2 4.1 %reshape.41 = bf16[32,4,7168]{2,1,0:T(4,128)(2,1)} reshape(bf16[128,7168]{1,0:T(8,128)(2,1)} %convolution_convert_fusion) | data formatting | bytes 3670016 | tf_op jit(solution)/shard_map/reshape | solution.py:31
  19.3 33.2 %all-gather.4.cloned.1.call-done = bf16[384,7168]{1,0:T(8,128)(2,1)} async-done(((bf16[96,7168]{1,0:T(8,128)(2,1)}), bf16[384,7168]{1,0:T(8,128)(2,1)}) %all-gather.4.cloned.1.call-update) | async-done | bytes 5505040 | tf_op jit(solution)/shard_map/all_gather | solution.py:39
  52.5 19.6 %fusion.15 = f32[384,2048]{1,0:T(8,128)} fusion(bf16[384,7168]{1,0:T(8,128)(2,1)} %all-gather.4.cloned.1.call-done, bf16[7168,2048]{1,0:T(8,128)(2,1)} %param.9), kind=kOutput, calls=%fused_computation.32 | convolution fusion | flops 11274289152 | bytes 38010880 | tf_op jit(solution)/shard_map/dot_general | solution.py:50
  72.2 160.0 %all-gather.6.cloned.1.call-done = bf16[32,7168,64]{1,2,0:T(8,128)(2,1)} async-done(((bf16[8,7168,64]{1,2,0:T(8,128)(2,1)}), bf16[32,7168,64]{1,2,0:T(8,128)(2,1)}) %all-gather.6.cloned.1.call-update) | async-done | bytes 29360144 | tf_op jit(solution)/shard_map/all_gather | solution.py:29
  232.1 13.6 %fusion.16 = f32[32,4,64]{2,1,0:T(4,128)S(1)} fusion(bf16[32,4,7168]{2,1,0:T(4,128)(2,1)} %reshape.41, bf16[32,7168,64]{1,2,0:T(8,128)(2,1)} %all-gather.6.cloned.1.call-done), kind=kOutput, calls=%fused_computation.33 | convolution fusion | flops 117440512 | bytes 31227904 | tf_op jit(solution)/shard_map/amf,afr->amr/dot_general | solution.py:32
  245.7 0.6 gather_fusion
  246.4 0.1 broadcast_select_fusion
  246.4 19.6 %psum.7 = bf16[96,64]{1,0:T(8,128)(2,1)S(1)} all-reduce(f32[96,64]{1,0:T(8,128)S(1)} %broadcast_select_fusion), channel_id=1, replica_groups=mesh['groups'=2,'tensor'=4,'store'=4] {'tensor'}, use_global_device_ids=true, to_apply=%region_2.3 | all-reduce | flops 6144 | bytes 36864 | tf_op jit(solution)/shard_map/psum | solution.py:35
  266.0 0.1 fusion.11
  266.1 0.1 copy.12
  266.2 5.2 %all-gather = bf16[4,96,16]{1,2,0:T(8,128)(2,1)S(1)} all-gather(bf16[1,96,16]{1,2,0:T(8,128)(2,1)S(1)} %copy.12), channel_id=1, replica_groups=mesh['groups'=2,'tensor'=4,'store'=4] {'store'}, dimensions={0}, use_global_device_ids=true | all-gather | bytes 15360 | tf_op jit(solution)/shard_map/all_gather | solution.py:40
  271.4 0.1 reshape.52
  271.5 0.0 copy-done
  271.5 5.4 %bitcast_add_fusion = f32[384,2048]{1,0:T(8,128)} fusion(f32[384,2048]{1,0:T(8,128)} %fusion.15, bf16[32,16,2048]{2,1,0:T(8,128)(2,1)S(1)} %copy-done, bf16[384,16]{0,1:T(8,128)(2,1)S(1)} %reshape.52, bf16[384,32]{0,1:T(8,128)(2,1)S(1)} %fusion.10), kind=kOutput, calls=%fused_computation.4 | convolution fusion | flops 806289408 | bytes 8425472 | tf_op jit(solution)/shard_map/dot_general | solution.py:52
  276.9 0.0 copy-start.2
  276.9 0.0 reduce-scatter.2.cloned.1.call-update
  276.9 58.6 %reduce-scatter.2.cloned.1.call-done = f32[96,2048]{1,0:T(8,128)} async-done(((f32[384,2048]{1,0:T(8,128)}), f32[96,2048]{1,0:T(8,128)}) %reduce-scatter.2.cloned.1.call-update) | async-done | bytes 786448 | tf_op jit(solution)/shard_map/reduce_scatter | solution.py:51
  335.5 0.0 copy-done.2
  335.5 2.0 add_convert_fusion
  (5 shorter events, 0.0 us)
Async XLA Ops:
  6.5 265.0 %copy-start = (bf16[32,16,2048]{2,1,0:T(8,128)(2,1)S(1)}, bf16[32,16,2048]{2,1,0:T(8,128)(2,1)}, u32[]{:S(2)}) copy-start(bf16[32,16,2048]{2,1,0:T(8,128)(2,1)} %param.11) | copy-start | bytes 6291460
  6.5 46.0 %all-gather.4.cloned.1.call-start = ((), (), s32[]{:S(2)}) async-start(), calls=%async_computation.1 | async-start | bytes 6881280 | tf_op jit(solution)/shard_map/all_gather | solution.py:39
  10.4 0.8 copy-start.3
  10.4 2.8 copy-start.1
  10.4 221.7 %all-gather.6.cloned.1.call-start = ((), (), s32[]{:S(2)}) async-start(), calls=%async_computation.2 | async-start | bytes 36700160 | tf_op jit(solution)/shard_map/all_gather | solution.py:29
  11.1 324.3 %reduce-scatter.2.cloned.1.call-start = ((), (), s32[]{:S(2)}) async-start(), calls=%async_computation.3 | async-start | bytes 3932160 | tf_op jit(solution)/shard_map/reduce_scatter | solution.py:51
  276.9 58.6 %copy-start.2 = (bf16[96,2048]{1,0:T(8,128)(2,1)S(1)}, bf16[96,2048]{1,0:T(8,128)(2,1)}, u32[]{:S(2)}) copy-start(bf16[96,2048]{1,0:T(8,128)(2,1)} %param.13) | copy-start | bytes 1179652
Sparse Core Ops, SparseCore 0:
  10.5 41.9 all-gather.3
  54.1 177.9 all-gather.5
  277.0 58.4 reduce-scatter.1
where the time goes:
time: 346 us; the launch traced here: 344 us
  waiting for transfers between devices  252 us (73%)
  matrix products  40.6 us (12%)
  blocking collectives  24.8 us (7%)
  between operations  13.2 us (4%)
  other arithmetic  7.77 us (2%)
  local copies, waits for them, and re-layouts  5.07 us (1%)
    all_gather x1, waiting for transfers between devices, shards(): partial_piece = lax.all_gather(shrink_weights, 'store', axis=0, tiled=True)  160 us
    reduce_scatter x1, waiting for transfers between devices, shards(): lax.psum_scatter(base + jnp.dot(expand_in, flattened_expand, preferred_el...  58.6 us
    all_gather x1, waiting for transfers between devices, shards(): lax.all_gather(hidden, 'store', axis=0, tiled=True)  33.2 us
    dot_general x1, matrix products, shards(): base = jnp.dot(hidden_all, down_weight, preferred_element_type=jnp.float32)  19.6 us
    psum x1, blocking collectives, shards(): summed = lax.psum(partial_value, 'tensor')  19.6 us
    dot_general x1, matrix products, shards(): jnp.einsum('amf,afr->amr', block, partial_piece, preferred_element_type=j...  13.6 us
  transfers between devices with their start and end apart: 3, of which 3 were waited for; matrix products, arithmetic and copies ran while one was open for 8% of the time, Pallas kernels for 0%

commit v1 on v0

v1 whole, which is shorter than its diff:
```python
import jax
import jax.numpy as jnp
from jax import lax
from jax.sharding import PartitionSpec as P


def shards(gate, up, down_weight, shrink_weights, expand_weights, row_adapter_index, residual):
    hidden = (jax.nn.silu(gate.astype(jnp.float32)) * up.astype(jnp.float32)).astype(jnp.bfloat16)
    adapters_here = shrink_weights.shape[0]
    adapter_table = expand_weights.shape[0]
    device_rank = expand_weights.shape[1]
    all_ids = row_adapter_index[:, 0]
    hidden_all = lax.all_gather(hidden, "store", axis=0, tiled=True)
    local = lax.axis_index("store") * adapters_here + jnp.arange(adapters_here, dtype=jnp.int32)
    part = jnp.einsum("rf,afk->ark", hidden_all, shrink_weights, preferred_element_type=jnp.float32)
    named = local[:, None] == all_ids[None, :]
    partial_value = jnp.sum(jnp.where(named[:, :, None], part, 0.0), axis=0)
    summed = lax.psum(partial_value, ("tensor", "store"))
    shrink_all = lax.dynamic_slice_in_dim(
        summed, lax.axis_index("tensor") * device_rank, device_rank, 1
    ).astype(jnp.bfloat16)
    flattened_expand = expand_weights.reshape(adapter_table * device_rank, expand_weights.shape[2])
    select = (all_ids[:, None] == jnp.arange(adapter_table, dtype=jnp.int32)[None, :]).astype(
        jnp.bfloat16
    )
    expand_in = (select[:, :, None] * shrink_all[:, None, :]).reshape(
        all_ids.shape[0], adapter_table * device_rank
    )
    base = jnp.dot(hidden_all, down_weight, preferred_element_type=jnp.float32)
    delta = jnp.dot(expand_in, flattened_expand, preferred_element_type=jnp.float32)
    total = lax.psum_scatter(
        (base + delta).astype(jnp.bfloat16), "tensor", scatter_dimension=0, tiled=True
    )
    return (residual.astype(jnp.float32) + total.astype(jnp.float32)).astype(jnp.bfloat16)


def solution(mesh):
    in_specs = (
        P(("groups", "store"), "tensor"),
        P(("groups", "store"), "tensor"),
        P("tensor", "store"),
        P("store", "tensor", None),
        P(None, "tensor", "store"),
        P("groups", None),
        P(("groups", "tensor"), "store"),
    )
    out_specs = P(("groups", "tensor"), "store")
    return jax.shard_map(shards, mesh=mesh, in_specs=in_specs, out_specs=out_specs, check_vma=False)
```

time: 346 us -> 186 us (0.54)
  waiting for transfers between devices: 252 us -> 79.1 us
  blocking collectives: 24.8 us -> 58.3 us
  matrix products: 40.6 us -> 27.9 us
  local copies, waits for them, and re-layouts: 5.07 us -> 0.02 us
    all_gather x2 -> x1, waiting for transfers between devices: 193 us -> 42 us  [shards(): hidden_all = lax.all_gather(hidden, 'store', axis=0, tiled=True)]
    psum x1, blocking collectives: 19.6 us -> 58.3 us  [shards(): summed = lax.psum(partial_value, ('tensor', 'store'))]
    reduce_scatter x1, waiting for transfers between devices: 58.6 us -> 37.1 us  [shards(): lax.psum_scatter((base + delta).astype(jnp.bfloat16), 'tensor', scatter_d...]
    dot_general x2 -> x0, matrix products: 15.6 us -> none  [the longest x1 13.6 us: shards(): jnp.einsum('amf,afr->amr', block, partial_piece, preferred_element_type=j...]
    unnamed x0 -> x1, matrix products: none -> 7.86 us
    all_gather x1 -> x0, blocking collectives: 5.19 us -> none  [shards(): lax.all_gather(shrink_low, 'store', axis=0, tiled=True)]
    reshape x1 -> x0, local copies, waits for them, and re-layouts: 4.08 us -> none  [shards(): block = packed.reshape(count, MOST, ffd)]
  transfers between devices with their start and end apart: 3 -> 2, of which waited for: 3 -> 2; matrix products, arithmetic and copies ran while one was open for 8% -> 0% of each run, Pallas kernels for 0% -> 0%
where the time goes in v1:
time: 186 us; the launch traced here: 185 us
  waiting for transfers between devices  79.1 us (43%)
  blocking collectives  58.3 us (31%)
  matrix products  27.9 us (15%)
  between operations  13.5 us (7%)
  other arithmetic  5.85 us (3%)
    psum x1, blocking collectives, shards(): summed = lax.psum(partial_value, ('tensor', 'store'))  58.3 us
    all_gather x1, waiting for transfers between devices, shards(): hidden_all = lax.all_gather(hidden, 'store', axis=0, tiled=True)  42 us
    reduce_scatter x1, waiting for transfers between devices, shards(): lax.psum_scatter((base + delta).astype(jnp.bfloat16), 'tensor', scatter_d...  37.1 us
    dot_general x1, matrix products, shards(): base = jnp.dot(hidden_all, down_weight, preferred_element_type=jnp.float32)  17.1 us
    unnamed x1, matrix products  7.86 us
    convert_element_type x1, other arithmetic, shards(): (jax.nn.silu(gate.astype(jnp.float32)) * up.astype(jnp.float32)).astype(j...  3.84 us
  transfers between devices with their start and end apart: 2, of which 2 were waited for; matrix products, arithmetic and copies ran while one was open for 0% of the time, Pallas kernels for 0%

profile of v1, /device:TPU:2, one launch (start us, length us, event | category | flops | bytes accessed | tf_op | source)
XLA Modules:
  0.0 184.7 jit_solution(10115251364236927489)
XLA Ops:
  6.5 0.0 copy-start
  6.5 0.0 copy-start.2
  6.5 0.0 all-gather.2.cloned.1.call-start
  6.5 3.8 %fusion.5 = bf16[96,7168]{1,0:T(8,128)(2,1)} fusion(bf16[96,7168]{1,0:T(8,128)(2,1)} %param.8, bf16[96,7168]{1,0:T(8,128)(2,1)} %param.7), kind=kLoop, calls=%fused_computation.8 | loop fusion | flops 5505024 | bytes 4128768 | tf_op jit(solution)/shard_map/convert_element_type | solution.py:8
  10.4 0.0 all-gather.2.cloned.1.call-update
  10.4 0.0 reduce-scatter.2.cloned.1.call-start
  10.5 0.0 copy-done.2
  10.5 0.1 broadcast_compare_fusion
  10.6 42.0 %all-gather.2.cloned.1.call-done = bf16[384,7168]{1,0:T(8,128)(2,1)} async-done(((bf16[96,7168]{1,0:T(8,128)(2,1)}), bf16[384,7168]{1,0:T(8,128)(2,1)}) %all-gather.2.cloned.1.call-update) | async-done | bytes 5505040 | tf_op jit(solution)/shard_map/all_gather | solution.py:13
  52.6 7.9 %fusion.12 = f32[384,512]{0,1:S(1)} fusion(bf16[384,7168]{1,0:T(8,128)(2,1)} %all-gather.2.cloned.1.call-done, bf16[7168,512]{0,1:T(8,128)(2,1)} %bitcast.15), kind=kOutput, calls=%fused_computation.21 | convolution fusion | flops 2818572288 | bytes 13631488
  60.4 0.1 select_reduce_fusion
  60.5 58.3 %psum.7 = bf16[384,64]{0,1:T(8,128)(2,1)S(1)} all-reduce(f32[384,64]{0,1:T(8,128)S(1)} %select_reduce_fusion), channel_id=1, replica_groups=mesh['groups'=2,'tensor'=4,'store'=4] {'tensor','store'}, use_global_device_ids=true, to_apply=%region_1.2 | all-reduce | flops 24576 | bytes 147456 | tf_op jit(solution)/shard_map/psum | solution.py:18
  118.8 17.1 %fusion.11 = f32[384,2048]{1,0:T(8,128)S(1)} fusion(bf16[384,7168]{1,0:T(8,128)(2,1)} %all-gather.2.cloned.1.call-done, bf16[7168,2048]{1,0:T(8,128)(2,1)} %param.9), kind=kOutput, calls=%fused_computation.20 | convolution fusion | flops 11274289152 | bytes 38010880 | tf_op jit(solution)/shard_map/dot_general | solution.py:29
  135.8 0.0 copy-done
  135.9 0.0 copy-start.1
  135.9 3.0 %fusion = bf16[384,2048]{1,0:T(8,128)(2,1)} fusion(f32[384,2048]{1,0:T(8,128)S(1)} %fusion.11, bf16[32,16,2048]{2,1,0:T(8,128)(2,1)S(1)} %copy-done, bf16[384,16]{0,1:T(8,128)(2,1)S(1)} %dynamic-slice_convert_fusion, bf16[384,32]{0,1:T(8,128)(2,1)S(1)} %fusion.10), kind=kOutput, calls=%fused_computation.3 | convolution fusion | flops 807075840 | bytes 6852608 | tf_op jit(solution)/shard_map/dot_general | solution.py:30
  138.8 0.0 reduce-scatter.2.cloned.1.call-update
  138.9 37.1 %reduce-scatter.2.cloned.1.call-done = bf16[96,2048]{1,0:T(8,128)(2,1)} async-done(((bf16[384,2048]{1,0:T(8,128)(2,1)}), bf16[96,2048]{1,0:T(8,128)(2,1)}) %reduce-scatter.2.cloned.1.call-update) | async-done | bytes 393232 | tf_op jit(solution)/shard_map/reduce_scatter | solution.py:31
  176.0 0.0 copy-done.1
  176.0 1.8 add_convert_fusion
  (4 shorter events, 0.0 us)
Async XLA Ops:
  6.5 129.3 %copy-start = (bf16[32,16,2048]{2,1,0:T(8,128)(2,1)S(1)}, bf16[32,16,2048]{2,1,0:T(8,128)(2,1)}, u32[]{:S(2)}) copy-start(bf16[32,16,2048]{2,1,0:T(8,128)(2,1)} %param.11) | copy-start | bytes 6291460
  6.5 3.9 %copy-start.2 = (s32[384,1]{0,1:T(1,128)S(1)}, s32[384,1]{0,1:T(1,128)}, u32[]{:S(2)}) copy-start(s32[384,1]{0,1:T(1,128)} %param.12) | copy-start | bytes 4612
  6.5 46.0 %all-gather.2.cloned.1.call-start = ((), (), s32[]{:S(2)}) async-start(), calls=%async_computation.1 | async-start | bytes 6881280 | tf_op jit(solution)/shard_map/all_gather | solution.py:13
  10.4 165.6 %reduce-scatter.2.cloned.1.call-start = ((), (), s32[]{:S(2)}) async-start(), calls=%async_computation.2 | async-start | bytes 1966080 | tf_op jit(solution)/shard_map/reduce_scatter | solution.py:31
  135.9 40.1 %copy-start.1 = (bf16[96,2048]{1,0:T(8,128)(2,1)S(1)}, bf16[96,2048]{1,0:T(8,128)(2,1)}, u32[]{:S(2)}) copy-start(bf16[96,2048]{1,0:T(8,128)(2,1)} %param.13) | copy-start | bytes 1179652
Sparse Core Ops, SparseCore 0:
  10.5 41.9 all-gather.1
  139.0 36.9 reduce-scatter.1

commit v2 on v1

--- a/solution.py
+++ b/solution.py
@@ -1,7 +1,332 @@
+import functools
 import jax
 import jax.numpy as jnp
 from jax import lax
+from jax.experimental import pallas as pl
+from jax.experimental.pallas import tpu as pltpu
 from jax.sharding import PartitionSpec as P
+
+PIECES = 2
+TILE = 512
+F32, BF16 = jnp.float32, jnp.bfloat16
+
+
+def kernel(T, pieces, *refs):
+    gate, up, down_hbm, shrink_hbm, expand_hbm, residual, ids_cols, ids_rows, out = refs[:9]
+    down, shrink, expand, hid, base, snd, from_left, from_right = refs[9:17]
+    parts, z_got, q_own, q_got = refs[17:21]
+    load_sem, h_send, h_recv, z_send, z_recv, q_send, q_recv, c_send, c_recv_l, c_recv_r = refs[21:]
+    rows, ffd = gate.shape
+    wide = down.shape[1]
+    piece = rows // pieces
+    rank = parts.shape[1]
+    adapters_here = shrink_hbm.shape[0] // rank
+    device_rank = rank // T
+    units = 2 * pieces
+
+    t = lax.axis_index("tensor")
+    s = lax.axis_index("store")
+    chip, core = s // 2, s % 2
+    sib = 2 * chip + 1 - core
+    peer = 2 * (1 - chip) + core
+    dia = 2 * (1 - chip) + 1 - core
+    left, right = (t + T - 1) % T, (t + 1) % T
+
+    loads = [
+        pltpu.make_async_copy(a, b, load_sem.at[i])
+        for i, (a, b) in enumerate(((shrink_hbm, shrink), (down_hbm, down), (expand_hbm, expand)))
+    ]
+    for load in loads:
+        load.start()
+
+    barrier = pltpu.get_barrier_semaphore()
+    for k in range(1, T):
+        pl.semaphore_signal(
+            barrier, inc=1, device_id={"tensor": (t + k) % T}, device_id_type=pl.DeviceIdType.MESH
+        )
+    for k in range(1, 4):
+        pl.semaphore_signal(
+            barrier, inc=1, device_id={"store": (s + k) % 4}, device_id_type=pl.DeviceIdType.MESH
+        )
+    pl.semaphore_wait(barrier, T - 1 + 3)
+
+    def remote(src, dst, send, recv, device):
+        return pltpu.make_async_remote_copy(
+            src_ref=src,
+            dst_ref=dst,
+            send_sem=send,
+            recv_sem=recv,
+            device_id=device,
+            device_id_type=pl.DeviceIdType.MESH,
+        )
+
+    def hidden_copy(kind, block, j, device):
+        ref = hid.at[block, pl.ds(j * piece, piece)]
+        return remote(ref, ref, h_send.at[kind, j], h_recv.at[kind, j], {"store": device})
+
+    step = 1024 if ffd % 1024 == 0 else ffd
+    for j in range(pieces):
+        here = slice(j * piece, (j + 1) * piece)
+
+        def columns(i, _, here=here):
+            at = pl.ds(pl.multiple_of(i * step, 128), step)
+            g = gate[here, at].astype(F32)
+            hid[s, here, at] = (g / (1.0 + jnp.exp(-g)) * up[here, at].astype(F32)).astype(BF16)
+            return 0
+
+        lax.fori_loop(0, ffd // step, columns, 0)
+        hidden_copy(0, s, j, peer).start()
+        hidden_copy(1, s, j, sib).start()
+
+    def unit_rows(u):
+        chip_of, j = (chip if u < pieces else 1 - chip), u % pieces
+        return 2 * chip_of, slice(j * piece, (j + 1) * piece), piece
+
+    def lhs(where):
+        first, here, n = where
+        return hid[pl.ds(first, 2), here, :].reshape(2 * n, ffd)
+
+    def shrink_part(u):
+        ids = ids_rows[u]
+        half = adapters_here // 2
+        total = None
+        for h in range(2):
+            part = lax.dot_general(
+                shrink[h * half * rank : (h + 1) * half * rank, :],
+                lhs(unit_rows(u)),
+                (((1,), (1,)), ((), ())),
+                preferred_element_type=F32,
+            )
+            for a in range(half):
+                mine = jnp.where(
+                    ids == s * adapters_here + h * half + a, part[a * rank : (a + 1) * rank], 0.0
+                )
+                total = mine if total is None else total + mine
+        parts[u] = total
+        for k in range(1, T):
+            z_copy(u, k).start()
+
+    def z_copy(u, k):
+        to = (t + k) % T
+        return remote(
+            parts.at[u, pl.ds(pl.multiple_of(to * device_rank, 8), device_rank)],
+            z_got.at[u, k - 1],
+            z_send.at[u, k - 1],
+            z_recv.at[u, k - 1],
+            {"tensor": to},
+        )
+
+    def q_copy(u, k):
+        to = u if k == 0 else (u + pieces) % units
+        return remote(
+            q_own.at[u], q_got.at[to, k], q_send.at[u, k], q_recv.at[to, k],
+            {"store": (sib, peer, dia)[k]},
+        )
+
+    def q_wait(u, k):
+        remote(
+            q_own.at[u], q_got.at[u, k], q_send.at[u, k], q_recv.at[u, k],
+            {"store": (sib, peer, dia)[k]},
+        ).wait_recv()
+
+    def shrink_sum(u):
+        total = parts[u, pl.ds(pl.multiple_of(t * device_rank, 8), device_rank), :]
+        for k in range(1, T):
+            z_copy(u, k).wait_recv()
+            total = total + z_got[u, k - 1]
+        q_own[u] = total
+        for k in range(3):
+            q_copy(u, k).start()
+
+    def product(where, lo, hi):
+        first, here, n = where
+
+        def tile(i, _):
+            at = pl.ds(pl.multiple_of(i * TILE, 128), TILE)
+            value = jnp.dot(lhs(where), down[:, at], preferred_element_type=F32)
+            base[pl.ds(first, 2), here, at] = value.reshape(2, n, TILE)
+            return 0
+
+        lax.fori_loop(lo, hi, tile, 0)
+
+    def delta(u):
+        first, here, n = unit_rows(u)
+        total = q_own[u]
+        for k in range(3):
+            q_wait(u, k)
+            total = total + q_got[u, k]
+        low = total.T.astype(BF16)
+        slots = expand.shape[0]
+        spread = (
+            lax.broadcasted_iota(jnp.int32, (device_rank, slots), 1) % device_rank
+            == lax.broadcasted_iota(jnp.int32, (device_rank, slots), 0)
+        )
+        wide_low = jnp.dot(low, jnp.where(spread, 1.0, 0.0).astype(BF16), preferred_element_type=F32)
+        named = (
+            lax.broadcasted_iota(jnp.int32, (2 * n, slots), 1) // device_rank == ids_cols[u]
+        )
+        expand_in = jnp.where(named, wide_low, 0.0).astype(BF16)
+
+        def tile(i, _):
+            at = pl.ds(pl.multiple_of(i * TILE, 128), TILE)
+            value = jnp.dot(expand_in, expand[:, at], preferred_element_type=F32)
+            base[pl.ds(first, 2), here, at] += value.reshape(2, n, TILE)
+            return 0
+
+        lax.fori_loop(0, wide // TILE, tile, 0)
+
+    def chain(u, i, to_right):
+        first, here, n = unit_rows(u)
+        place = (first + i, pl.ds(here.start, n))
+        into = from_left if to_right else from_right
+        got = c_recv_l if to_right else c_recv_r
+        return remote(
+            snd.at[place], into.at[place], c_send.at[u, i], got.at[u, i],
+            {"tensor": right if to_right else left},
+        )
+
+    def hop(u, middle):
+        first, here, n = unit_rows(u)
+        for i in range(2):
+            b = first + i
+            for to_right in (True, False):
+                onward = (t < b) if to_right else (t > b)
+                end = (t == 0) if to_right else (t == T - 1)
+                inner = (t > 0) if to_right else (t < T - 1)
+
+                @pl.when(onward & (inner if middle else end))
+                def _(i=i, b=b, to_right=to_right):
+                    value = base[b, here, :]
+                    if middle:
+                        chain(u, i, to_right).wait_recv()
+                        got = from_left if to_right else from_right
+                        value = value + got[b, here, :].astype(F32)
+                    snd[b, here, :] = value.astype(BF16)
+                    chain(u, i, to_right).start()
+
+    def finish(u):
+        first, here, n = unit_rows(u)
+        for i in range(2):
+            b = first + i
+
+            @pl.when(t == b)
+            def _(i=i, b=b):
+                base[b, here, :] += residual[here, :].astype(F32)
+
+                @pl.when(t > 0)
+                def _():
+                    chain(u, i, True).wait_recv()
+                    base[b, here, :] += from_left[b, here, :].astype(F32)
+
+                @pl.when(t < T - 1)
+                def _():
+                    chain(u, i, False).wait_recv()
+                    base[b, here, :] += from_right[b, here, :].astype(F32)
+
+                out[here, :] = base[b, here, :].astype(BF16)
+
+            @pl.when(t != b)
+            def _(i=i):
+                chain(u, i, True).wait_send()
+
+    tiles = wide // TILE
+    near = (2 * chip, slice(0, rows), rows)
+    for j in range(pieces):
+        hidden_copy(1, sib, j, sib).wait_recv()
+    loads[0].wait()
+    for j in range(pieces):
+        shrink_part(j)
+    loads[1].wait()
+    product(near, 0, tiles // 2)
+    for j in range(pieces):
+        shrink_sum(j)
+    product(near, tiles // 2, tiles)
+    loads[2].wait()
+    for j in range(pieces):
+        u = pieces + j
+        hidden_copy(0, peer, j, peer).wait_recv()
+        hidden_copy(2, peer, j, sib).start()
+        hidden_copy(2, dia, j, sib).wait_recv()
+        shrink_part(u)
+        product(unit_rows(u), 0, tiles // 2)
+        shrink_sum(u)
+        if j > 0:
+            hop(j - 1, True)
+            hop(u - 1, True)
+        product(unit_rows(u), tiles // 2, tiles)
+        delta(j)
+        hop(j, False)
+        delta(u)
+        hop(u, False)
+    hop(pieces - 1, True)
+    hop(units - 1, True)
+    for u in range(units):
+        finish(u)
+    for j in range(pieces):
+        hidden_copy(0, s, j, peer).wait_send()
+        hidden_copy(1, s, j, sib).wait_send()
+        hidden_copy(2, peer, j, sib).wait_send()
+    for u in range(units):
+        for k in range(1, T):
+            z_copy(u, k).wait_send()
+        for k in range(3):
+            q_copy(u, k).wait_send()
+
+
+def fused(T, gate, up, down_weight, shrink_weights, expand_weights, row_adapter_index, residual):
+    rows, ffd = gate.shape
+    wide = down_weight.shape[1]
+    adapters_here, _, rank = shrink_weights.shape
+    table, device_rank, _ = expand_weights.shape
+    pieces = PIECES
+    piece = rows // pieces
+    shrink = jnp.swapaxes(shrink_weights, 1, 2).reshape(adapters_here * rank, ffd)
+    expand = expand_weights.reshape(table * device_rank, wide)
+    chip = lax.axis_index("store") // 2
+    ids = row_adapter_index.reshape(2, 2, pieces, piece)
+    ids = jnp.where(chip == 0, ids, ids[::-1]).transpose(0, 2, 1, 3).reshape(2 * pieces, 2 * piece)
+    units = 2 * pieces
+    vmem = pl.BlockSpec(memory_space=pltpu.VMEM)
+    hbm = pl.BlockSpec(memory_space=pl.ANY)
+    dma = pltpu.SemaphoreType.DMA
+    return pl.pallas_call(
+        functools.partial(kernel, T, pieces),
+        out_shape=jax.ShapeDtypeStruct((rows, wide), BF16),
+        in_specs=[vmem, vmem, hbm, hbm, hbm, vmem] + [vmem, vmem],
+        out_specs=vmem,
+        scratch_shapes=[
+            pltpu.VMEM((ffd, wide), BF16),
+            pltpu.VMEM((adapters_here * rank, ffd), BF16),
+            pltpu.VMEM((table * device_rank, wide), BF16),
+            pltpu.VMEM((4, rows, ffd), BF16),
+            pltpu.VMEM((4, rows, wide), F32),
+            pltpu.VMEM((4, rows, wide), BF16),
+            pltpu.VMEM((4, rows, wide), BF16),
+            pltpu.VMEM((4, rows, wide), BF16),
+        ]
+        + [
+            pltpu.VMEM((units, rank, 2 * piece), F32),
+            pltpu.VMEM((units, T - 1, device_rank, 2 * piece), F32),
+            pltpu.VMEM((units, device_rank, 2 * piece), F32),
+            pltpu.VMEM((units, 3, device_rank, 2 * piece), F32),
+            dma((3,)),
+            dma((3, pieces)),
+            dma((3, pieces)),
+            dma((units, T - 1)),
+            dma((units, T - 1)),
+            dma((units, 3)),
+            dma((units, 3)),
+            dma((units, 2)),
+            dma((units, 2)),
+            dma((units, 2)),
+        ],
+        compiler_params=pltpu.CompilerParams(
+            collective_id=0, has_side_effects=True, vmem_limit_bytes=62 * 2**20
+        ),
+    )(
+        gate, up, down_weight, shrink, expand, residual,
+        ids[:, :, None], ids[:, None, :],
+    )
 
 
 def shards(gate, up, down_weight, shrink_weights, expand_weights, row_adapter_index, residual):
@@ -35,6 +360,7 @@
 
 
 def solution(mesh):
+    tensor, store = mesh.shape["tensor"], mesh.shape["store"]
     in_specs = (
         P(("groups", "store"), "tensor"),
         P(("groups", "store"), "tensor"),
@@ -45,4 +371,5 @@
         P(("groups", "tensor"), "store"),
     )
     out_specs = P(("groups", "tensor"), "store")
-    return jax.shard_map(shards, mesh=mesh, in_specs=in_specs, out_specs=out_specs, check_vma=False)
+    body = functools.partial(fused, tensor) if tensor == 4 and store == 4 else shards
+    return jax.shard_map(body, mesh=mesh, in_specs=in_specs, out_specs=out_specs, check_vma=False)

time: 186 us -> 97.9 us (0.53)
  Pallas kernels: 0 us -> 93.7 us
  waiting for transfers between devices: 79.1 us -> 0 us
  blocking collectives: 58.3 us -> 0 us
  matrix products: 27.9 us -> 0 us
  between operations: 13.5 us -> 0.02 us
  other arithmetic: 5.85 us -> 0.7 us
  local copies, waits for them, and re-layouts: 0.02 us -> 3.32 us
    pallas_call x0 -> x1, Pallas kernels: none -> 93.7 us  [fused(): pl.pallas_call(functools.partial(kernel, T, pieces), out_shape=jax.ShapeD...]
    psum x1 -> x0, blocking collectives: 58.3 us -> none  [shards(): summed = lax.psum(partial_value, ('tensor', 'store'))]
    all_gather x1 -> x0, waiting for transfers between devices: 42 us -> none  [shards(): hidden_all = lax.all_gather(hidden, 'store', axis=0, tiled=True)]
    reduce_scatter x1 -> x0, waiting for transfers between devices: 37.1 us -> none  [shards(): lax.psum_scatter((base + delta).astype(jnp.bfloat16), 'tensor', scatter_d...]
    dot_general x2 -> x0, matrix products: 20 us -> none  [the longest x1 17.1 us: shards(): base = jnp.dot(hidden_all, down_weight, preferred_element_type=jnp.float32)]
    unnamed x1 -> x0, matrix products: 7.86 us -> none
    convert_element_type x3 -> x0, other arithmetic: 5.69 us -> none  [the longest x1 3.84 us: shards(): (jax.nn.silu(gate.astype(jnp.float32)) * up.astype(jnp.float32)).astype(j...]
  transfers between devices with their start and end apart: 2 -> 0, of which waited for: 2 -> 0; matrix products, arithmetic and copies ran while one was open for 0% -> 0% of each run, Pallas kernels for 0% -> 0%
where the time goes in v2:
time: 97.9 us; the launch traced here: 97.7 us
  Pallas kernels  93.7 us (96%)
  local copies, waits for them, and re-layouts  3.32 us (3%)
    pallas_call x1, Pallas kernels, fused(): pl.pallas_call(functools.partial(kernel, T, pieces), out_shape=jax.ShapeD...  93.7 us

profile of v2, /device:TPU:2, one launch (start us, length us, event | category | flops | bytes accessed | tf_op | source)
XLA Modules:
  0.0 97.7 jit_solution(10815370728586575339)
XLA Ops:
  0.0 0.7 reduce
  0.7 0.1 reshape.11
  0.8 0.7 broadcast_in_dim_reshape.7.refs_7_
  1.5 0.8 broadcast_in_dim_reshape.8.refs_6_
  2.3 93.7 %shard_map.73 = bf16[96,2048]{1,0:T(8,128)(2,1)} custom-call(bf16[96,7168]{1,0:T(8,128)(2,1)} %refs_0_.1, bf16[96,7168]{1,0:T(8,128)(2,1)} %refs_1_.1, bf16[7168,2048]{1,0:T(8,128)(2,1)} %refs_2_.1, bf16[512,7168]{1,0:T(8,128)(2,1)} %bitcast.6, bf16[512,2048]{1,0:T(8,128)(2,1)} %bitcast.7, bf16[96,2048]{1,0:T(8,128)(2,1)} %refs_5_.1, ...), custom_call_target="tpu_custom_call" | custom-call | tf_op jit(solution)/shard_map/pallas_call | solution.py:292
  96.0 1.8 %copy.14 = bf16[96,2048]{1,0:T(8,128)(2,1)} copy(bf16[96,2048]{1,0:T(8,128)(2,1)} %shard_map.73) | data formatting | bytes 786432
  (2 shorter events, 0.0 us)
